TPU v7x, 32 devices: a whole 2x2x4 slice. The times are simulated.
32 devices in a mesh: grp: 4 (over y, x), seq: 8 (over z, core).
Axes of the slice: x: 2, y: 2, z: 4, core: 2. Of those that a mesh axis runs over, the one named last changes fastest.
Arguments:
- tiles: bfloat16 [8, 4096, 768], P('grp', 'seq'), may hold values from -8 to 8
- counts: int32 [8], P('grp'), may hold values from 1024 to 4096, as said below
- ln1_gain: float32 [768], replicated, may hold values from 0.1 to 1.9
- qkv_weight: bfloat16 [768, 2304], replicated, may hold values from -0.18042196 to 0.18042196
- out_weight: bfloat16 [768, 768], replicated, may hold values from -0.21875 to 0.21875
- ln2_gain: float32 [768], replicated, may hold values from 0.1 to 1.9
- ff_in: bfloat16 [768, 3072], replicated, may hold values from -0.21875 to 0.21875
- ff_out: bfloat16 [3072, 768], replicated, may hold values from -0.109375 to 0.109375
- pool_weight: bfloat16 [768, 768], P('grp'), may hold values from -0.18042196 to 0.18042196
- class_weight: float32 [384, 8], replicated, may hold values from -3 to 6
Outputs:
- encoded: bfloat16 [8, 4096, 768], P('grp', 'seq')
- pooled: float32 [8, 8, 768], P('grp')
Inputs may be any that keep to these rules, and one draw needn't show every extreme that they name: The valid tiles of a slide are its first counts tiles in scan order; some slide has all 4096 tiles valid.
All inputs are finite; a program needn't handle non-finite values.
Results may differ from a plain program's by a relative error of at most 0.015.
Values may be sent and summed in bfloat16 or wider, within the bound.
A program may use at most 128 MiB of HBM per device.

v0:
```python
import functools
import math

import jax
import jax.numpy as jnp
from jax import lax
from jax.experimental import pallas as pl
from jax.experimental.pallas import tpu as pltpu
from jax.sharding import PartitionSpec as P

HEADS = 16
BLOCK = 256
AUG = 16
NEG = -1e30
NT = (((1,), (1,)), ((), ()))
TN = (((0,), (0,)), ((), ()))


def normalize(xf, gain):
    centre = jnp.mean(xf, axis=-1, keepdims=True)
    spread = jnp.mean((xf - centre) ** 2, axis=-1, keepdims=True)
    return (xf - centre) * lax.rsqrt(spread + 1e-05) * gain


def spread_matrix(rows, ratio):
    chunk = rows // ratio
    r = lax.broadcasted_iota(jnp.int32, (rows, rows), 0)
    t = lax.broadcasted_iota(jnp.int32, (rows, rows), 1)
    return jnp.where((r % chunk) * ratio + r // chunk == t, 1.0, 0.0)


def attend(kt, qt, vt, head_dim):
    scale = 1.0 / head_dim**0.5
    c = scale * math.log2(math.e)
    s = lax.dot_general(kt, qt, TN, preferred_element_type=jnp.float32)
    m = jnp.max(s, axis=0, keepdims=True)
    p = jnp.exp2((s - m) * c).astype(jnp.bfloat16)
    o = jnp.dot(vt, p, preferred_element_type=jnp.float32)
    total = o[head_dim : head_dim + 1]
    return o[:head_dim] / total, m * scale + jnp.log(total)


def attention_kernel(
    ratio,
    counts_ref,
    tiles_ref,
    gain_ref,
    w_ref,
    mixed_ref,
    wt,
    spread_ref,
    x_near,
    x_send,
    x_recv,
    proj,
    near_out,
    near_lse,
    o_t,
    l_t,
    o_send,
    o_recv,
    l_send,
    l_recv,
    l_rows,
    x_ss,
    x_rs,
    o_ss,
    o_rs,
    l_ss,
    l_rs,
):
    me = lax.axis_index("seq")
    slides, rows, width = tiles_ref.shape
    head_dim = width // HEADS
    nblocks = rows // BLOCK
    chunk = rows // ratio

    def x_copy(s, peer):
        return pltpu.make_async_remote_copy(
            src_ref=x_send.at[s, peer],
            dst_ref=x_recv.at[s, me],
            send_sem=x_ss.at[s, peer],
            recv_sem=x_rs.at[s, me],
            device_id={"seq": peer},
            device_id_type=pl.DeviceIdType.MESH,
        )

    def x_arrival(s, peer):
        return pltpu.make_async_remote_copy(
            src_ref=x_send.at[s, peer],
            dst_ref=x_recv.at[s, peer],
            send_sem=x_ss.at[s, peer],
            recv_sem=x_rs.at[s, peer],
            device_id={"seq": peer},
            device_id_type=pl.DeviceIdType.MESH,
        )

    def o_copy(s, peer, slot):
        return pltpu.make_async_remote_copy(
            src_ref=o_send.at[s, peer],
            dst_ref=o_recv.at[s, slot],
            send_sem=o_ss.at[s, peer],
            recv_sem=o_rs.at[s, slot],
            device_id={"seq": peer},
            device_id_type=pl.DeviceIdType.MESH,
        )

    def l_copy(s, peer, slot):
        return pltpu.make_async_remote_copy(
            src_ref=l_send.at[s, peer],
            dst_ref=l_recv.at[s, slot],
            send_sem=l_ss.at[s, peer],
            recv_sem=l_rs.at[s, slot],
            device_id={"seq": peer},
            device_id_type=pl.DeviceIdType.MESH,
        )

    def partner(k):
        return lax.rem(me + k, ratio)

    barrier = pltpu.get_barrier_semaphore()
    for k in range(1, ratio):
        pl.semaphore_signal(
            barrier, inc=1, device_id={"seq": partner(k)}, device_id_type=pl.DeviceIdType.MESH
        )

    spread_ref[...] = spread_matrix(rows, ratio).astype(jnp.bfloat16)
    for s in range(slides):
        xf = tiles_ref[s].astype(jnp.float32)
        normed = normalize(xf, gain_ref[...]).astype(jnp.bfloat16)
        x_near[s] = normed
        moved = jnp.dot(spread_ref[...], normed, preferred_element_type=jnp.float32)
        x_send[s] = moved.astype(jnp.bfloat16).reshape(ratio, chunk, width)
        if s == 0:
            pl.semaphore_wait(barrier, ratio - 1)

        def send(k, carry, s=s):
            x_copy(s, partner(k)).start()
            return carry

        lax.fori_loop(1, ratio, send, 0)

    for j in range(3):
        wt[j] = w_ref[:, j * width : (j + 1) * width].T
    first = lax.broadcasted_iota(jnp.int32, (AUG, rows), 0) == 0
    lane = lax.broadcasted_iota(jnp.int32, (AUG, rows), 1)
    ones = jnp.where(first, 1.0, 0.0).astype(jnp.bfloat16)
    for h in range(HEADS):
        proj[0, h, head_dim:, :] = ones
        proj[2, h, head_dim:, :] = ones

    def project(x, keep):
        bias = jnp.where(first & jnp.logical_not(keep), NEG, 0.0).astype(jnp.bfloat16)
        for h in range(HEADS):
            proj[1, h, head_dim:, :] = bias

        def part(j, carry):
            y = lax.dot_general(wt[j], x, NT, preferred_element_type=jnp.float32)
            proj[j, :, :head_dim, :] = y.astype(jnp.bfloat16).reshape(HEADS, head_dim, rows)
            return carry

        lax.fori_loop(0, 3, part, 0)

    local_pos = me * rows + lane

    def near(s, carry):
        project(x_near[s], local_pos < counts_ref[s])

        def head(h, carry):
            for b in range(nblocks):
                cols = slice(b * BLOCK, (b + 1) * BLOCK)
                out, lse = attend(
                    proj[1, h, :, cols], proj[0, h, :, cols], proj[2, h, :, cols], head_dim
                )
                near_out[s, h, :, cols] = out
                near_lse[s, h, :, cols] = lse
            return carry

        lax.fori_loop(0, HEADS, head, 0, unroll=4)
        return carry

    lax.fori_loop(0, slides, near, 0)

    class_pos = lane * ratio + me

    def far(s, carry):
        def arrive(k, carry):
            x_arrival(s, partner(k)).wait_recv()
            return carry

        lax.fori_loop(1, ratio, arrive, 0)
        x_recv[s, me] = x_send[s, me]
        project(x_recv[s].reshape(rows, width), class_pos < counts_ref[s])

        def head(h, carry):
            out, lse = attend(proj[1, h], proj[0, h], proj[2, h], head_dim)
            o_t[h] = out.astype(jnp.bfloat16)
            l_t[h] = lse
            return carry

        lax.fori_loop(0, HEADS, head, 0, unroll=2)
        o_send[s] = o_t[...].reshape(width, rows).T.reshape(ratio, chunk, width)
        lse = l_t[...].reshape(HEADS, rows)
        for d in range(ratio):
            l_send[s, d] = lse[:, d * chunk : (d + 1) * chunk]

        def send(k, carry):
            o_copy(s, partner(k), me).start()
            l_copy(s, partner(k), me).start()
            return carry

        lax.fori_loop(1, ratio, send, 0)
        return carry

    lax.fori_loop(0, slides, far, 0)

    def mix(s, carry):
        def arrive(k, carry):
            o_copy(s, partner(k), partner(k)).wait_recv()
            l_copy(s, partner(k), partner(k)).wait_recv()
            return carry

        lax.fori_loop(1, ratio, arrive, 0)
        o_recv[s, me] = o_send[s, me]
        l_recv[s, me] = l_send[s, me]
        for c in range(ratio):
            l_rows[c] = l_recv[s, c].T
        far_lse = jnp.dot(
            l_rows[...].reshape(rows, HEADS).T,
            spread_ref[...].astype(jnp.float32),
            precision=lax.Precision.HIGHEST,
            preferred_element_type=jnp.float32,
        ).reshape(HEADS, 1, rows)
        n_lse = near_lse[s]
        top = jnp.maximum(n_lse, far_lse)
        n_w = jnp.exp(n_lse - top)
        f_w = jnp.exp(far_lse - top)
        inv = 1.0 / (n_w + f_w)
        n_w = n_w * inv
        f_w = f_w * inv
        far_out = lax.dot_general(
            o_recv[s].reshape(rows, width),
            spread_ref[...],
            TN,
            preferred_element_type=jnp.float32,
        ).reshape(HEADS, head_dim, rows)
        mixed = (n_w * near_out[s] + f_w * far_out).astype(jnp.bfloat16)
        mixed_ref[s] = mixed.reshape(width, rows).T
        return carry

    lax.fori_loop(0, slides, mix, 0)

    def drain(i, carry):
        s = i // (ratio - 1)
        peer = partner(i % (ratio - 1) + 1)
        x_copy(s, peer).wait_send()
        o_copy(s, peer, me).wait_send()
        l_copy(s, peer, me).wait_send()
        return carry

    lax.fori_loop(0, slides * (ratio - 1), drain, 0)


def attention(tiles, counts, gain, qkv_weight, ratio):
    slides, rows, width = tiles.shape
    head_dim = width // HEADS
    chunk = rows // ratio
    bf16, f32 = jnp.bfloat16, jnp.float32
    vmem = pl.BlockSpec(memory_space=pltpu.VMEM)
    sem = pltpu.SemaphoreType.DMA((slides, ratio))
    return pl.pallas_call(
        functools.partial(attention_kernel, ratio),
        out_shape=jax.ShapeDtypeStruct((slides, rows, width), bf16),
        in_specs=[pl.BlockSpec(memory_space=pltpu.SMEM), vmem, vmem, vmem],
        out_specs=vmem,
        scratch_shapes=[
            pltpu.VMEM((3, width, width), bf16),
            pltpu.VMEM((rows, rows), bf16),
            pltpu.VMEM((slides, rows, width), bf16),
            pltpu.VMEM((slides, ratio, chunk, width), bf16),
            pltpu.VMEM((slides, ratio, chunk, width), bf16),
            pltpu.VMEM((3, HEADS, head_dim + AUG, rows), bf16),
            pltpu.VMEM((slides, HEADS, head_dim, rows), f32),
            pltpu.VMEM((slides, HEADS, 1, rows), f32),
            pltpu.VMEM((HEADS, head_dim, rows), bf16),
            pltpu.VMEM((HEADS, 1, rows), f32),
            pltpu.VMEM((slides, ratio, chunk, width), bf16),
            pltpu.VMEM((slides, ratio, chunk, width), bf16),
            pltpu.VMEM((slides, ratio, HEADS, chunk), f32),
            pltpu.VMEM((slides, ratio, HEADS, chunk), f32),
            pltpu.VMEM((ratio, chunk, HEADS), f32),
            sem,
            sem,
            sem,
            sem,
            sem,
            sem,
        ],
        compiler_params=pltpu.CompilerParams(
            collective_id=0, has_side_effects=True, vmem_limit_bytes=48 * 2**20
        ),
        cost_estimate=pl.CostEstimate(
            flops=2 * slides * rows * width * width * 8,
            bytes_accessed=8 * slides * rows * width,
            transcendentals=0,
        ),
    )(counts, tiles, gain.reshape(1, width), qkv_weight)


def gelu(x):
    return 0.5 * x * (1.0 + lax.erf(x * math.sqrt(0.5)))


def feed_kernel(
    counts_ref,
    tiles_ref,
    mixed_ref,
    wo_ref,
    gain_ref,
    fi_ref,
    fo_ref,
    pw_ref,
    cw_ref,
    enc_ref,
    stat_ref,
    peak_s,
    total_s,
    numer_s,
):
    s = pl.program_id(0)
    t = pl.program_id(1)
    here = lax.axis_index("seq")
    size, width = mixed_ref.shape[1:]
    f32, bf16 = jnp.float32, jnp.bfloat16
    start = here * size * pl.num_programs(1) + t * size
    count = counts_ref[s]
    resid = tiles_ref[0].astype(f32) + jnp.dot(
        mixed_ref[0], wo_ref[...], preferred_element_type=f32
    )
    normed = normalize(resid, gain_ref[...]).astype(bf16)
    ff = fi_ref.shape[1]
    step = width
    out = resid
    for j in range(0, ff, step):
        h = jnp.dot(normed, fi_ref[:, j : j + step], preferred_element_type=f32)
        act = gelu(h).astype(bf16)
        out = out + jnp.dot(act, fo_ref[j : j + step, :], preferred_element_type=f32)
    rowpos = start + lax.broadcasted_iota(jnp.int32, (size, width), 0)
    encoded = jnp.where(rowpos < count, out, 0.0).astype(bf16)
    enc_ref[0] = encoded
    zed = jnp.dot(encoded, pw_ref[...], preferred_element_type=f32)
    hidden = zed.shape[1] // 2
    gate = jnp.tanh(zed[:, :hidden]) * jax.nn.sigmoid(zed[:, hidden:])
    logits = lax.dot_general(
        cw_ref[...], gate, NT, precision=lax.Precision.HIGHEST, preferred_element_type=f32
    )
    classes = logits.shape[0]
    keep = start + lax.broadcasted_iota(jnp.int32, (classes, size), 1) < count
    logits = jnp.where(keep, logits, NEG)

    @pl.when(t == 0)
    def _():
        peak_s[...] = jnp.full_like(peak_s, NEG)
        total_s[...] = jnp.zeros_like(total_s)
        numer_s[...] = jnp.zeros_like(numer_s)

    old = peak_s[:, :1]
    peak = jnp.maximum(old, jnp.max(logits, axis=1, keepdims=True))
    fade = jnp.exp(old - peak)
    expo = jnp.where(keep, jnp.exp(logits - peak), 0.0)
    numer = jnp.dot(
        expo, encoded.astype(f32), precision=lax.Precision.HIGHEST, preferred_element_type=f32
    )
    total_s[...] = total_s[...] * fade + jnp.sum(expo, axis=1, keepdims=True)
    numer_s[...] = numer_s[...] * fade + numer
    peak_s[...] = jnp.broadcast_to(peak, peak_s.shape)

    @pl.when(t == pl.num_programs(1) - 1)
    def _():
        stat_ref[0, :, :width] = numer_s[...]
        stat_ref[0, :, width : width + 128] = total_s[...]
        stat_ref[0, :, width + 128 :] = peak_s[...]


def feed(counts, tiles, mixed, wo, gain, fi, fo, pw, cw):
    slides, rows, width = tiles.shape
    size = min(512, rows)
    classes = cw.shape[0]
    f32 = jnp.float32

    def whole(a):
        return pl.BlockSpec(a.shape, lambda s, t: (0, 0))

    gain = gain.reshape(1, width)
    block = pl.BlockSpec((1, size, width), lambda s, t: (s, t, 0))
    return pl.pallas_call(
        feed_kernel,
        grid=(slides, rows // size),
        out_shape=(
            jax.ShapeDtypeStruct(tiles.shape, tiles.dtype),
            jax.ShapeDtypeStruct((slides, classes, width + 256), f32),
        ),
        in_specs=[
            pl.BlockSpec(memory_space=pltpu.SMEM),
            block,
            block,
            whole(wo),
            whole(gain),
            whole(fi),
            whole(fo),
            whole(pw),
            whole(cw),
        ],
        out_specs=(block, pl.BlockSpec((1, classes, width + 256), lambda s, t: (s, 0, 0))),
        scratch_shapes=[
            pltpu.VMEM((classes, 128), f32),
            pltpu.VMEM((classes, 128), f32),
            pltpu.VMEM((classes, width), f32),
        ],
        compiler_params=pltpu.CompilerParams(vmem_limit_bytes=56 * 2**20),
        cost_estimate=pl.CostEstimate(
            flops=2 * slides * rows * width * (2 * width + 2 * fi.shape[1]),
            bytes_accessed=8 * slides * rows * width,
            transcendentals=0,
        ),
    )(counts, tiles, mixed, wo, gain, fi, fo, pw, cw)


def pool_kernel(ratio, stat_ref, out_ref, got, ss, rs):
    me = lax.axis_index("seq")
    width = out_ref.shape[-1]

    def copy(peer, slot):
        return pltpu.make_async_remote_copy(
            src_ref=stat_ref,
            dst_ref=got.at[slot],
            send_sem=ss.at[peer],
            recv_sem=rs.at[slot],
            device_id={"seq": peer},
            device_id_type=pl.DeviceIdType.MESH,
        )

    def partner(k):
        return lax.rem(me + k, ratio)

    barrier = pltpu.get_barrier_semaphore()
    for k in range(1, ratio):
        pl.semaphore_signal(
            barrier, inc=1, device_id={"seq": partner(k)}, device_id_type=pl.DeviceIdType.MESH
        )
    pl.semaphore_wait(barrier, ratio - 1)

    def send(k, carry):
        copy(partner(k), me).start()
        return carry

    lax.fori_loop(1, ratio, send, 0)
    got[me] = stat_ref[...]

    def arrive(k, carry):
        copy(partner(k), partner(k)).wait_recv()
        return carry

    lax.fori_loop(1, ratio, arrive, 0)
    peaks = got[:, :, :, width + 128 :]
    peak = jnp.max(peaks, axis=0)
    fade = jnp.exp(peaks - peak[None])
    total = jnp.sum(got[:, :, :, width : width + 128] * fade, axis=0)
    inv = 1.0 / total
    for j in range(0, width, 128):
        numer = jnp.sum(got[:, :, :, j : j + 128] * fade, axis=0)
        out_ref[:, :, j : j + 128] = numer * inv

    def drain(k, carry):
        copy(partner(k), me).wait_send()
        return carry

    lax.fori_loop(1, ratio, drain, 0)


def pool(stat, width, ratio):
    slides, classes, _ = stat.shape
    vmem = pl.BlockSpec(memory_space=pltpu.VMEM)
    return pl.pallas_call(
        functools.partial(pool_kernel, ratio),
        out_shape=jax.ShapeDtypeStruct((slides, classes, width), jnp.float32),
        in_specs=[vmem],
        out_specs=vmem,
        scratch_shapes=[
            pltpu.VMEM((ratio,) + stat.shape, jnp.float32),
            pltpu.SemaphoreType.DMA((ratio,)),
            pltpu.SemaphoreType.DMA((ratio,)),
        ],
        compiler_params=pltpu.CompilerParams(collective_id=1, has_side_effects=True),
    )(stat)


def local(
    tiles,
    counts,
    ln1_gain,
    qkv_weight,
    out_weight,
    ln2_gain,
    ff_in,
    ff_out,
    pool_weight,
    class_weight,
):
    ratio = lax.axis_size("seq")
    pw = lax.all_gather(pool_weight, "grp", axis=0, tiled=True)
    mixed = attention(tiles, counts, ln1_gain, qkv_weight, ratio)
    encoded, stat = feed(
        counts, tiles, mixed, out_weight, ln2_gain, ff_in, ff_out, pw, class_weight.T
    )
    pooled = pool(stat, tiles.shape[-1], ratio)
    return (encoded, pooled)


def solution(mesh):
    placed = (P("grp", "seq", None), P("grp"), P(), P(), P(), P(), P(), P(), P("grp", None), P())
    return jax.shard_map(
        local,
        mesh=mesh,
        in_specs=placed,
        out_specs=(P("grp", "seq", None), P("grp", None, None)),
        check_vma=False,
    )
```

profile of v0, /device:TPU:0, one launch (start us, length us, event | category | flops | bytes accessed | tf_op | source)
XLA Modules:
  0.0 142.0 jit_solution(2692018782982211041)
XLA Ops:
  7.2 0.0 all-gather.2.cloned.1.call-start
  7.2 0.7 all-gather.2.cloned.1.call-update
  7.9 0.7 reshape.10.gain_ref
  8.6 1.3 reshape.11.gain_ref
  9.9 0.0 copy-start
  9.9 1.4 copy-done
  11.3 0.0 copy-start.1
  11.3 0.7 copy-done.1
  11.9 78.4 %shard_map.113.mixed_ref = bf16[2,512,768]{2,1,0:T(8,128)(2,1)S(1)} custom-call(s32[2]{0:T(128)S(1)} %copy-done.1, bf16[2,512,768]{2,1,0:T(8,128)(2,1)S(1)} %copy-done, f32[1,768]{1,0:T(1,128)S(1)} %reshape.10.gain_ref, bf16[768,2304]{1,0:T(8,128)(2,1)} %w_ref.1), custom_call_target="tpu_custom_call" | custom-call | flops 9663676416 | bytes 6291456 | tf_op jit(solution)/shard_map/pallas_call | solution.py:271
  90.3 0.0 copy-start.2
  90.3 1.1 copy-done.2
  91.5 0.0 all-gather.2.cloned.1.call-done.pw_ref
  91.5 22.9 %shard_map.114 = (bf16[2,512,768]{2,1,0:T(8,128)(2,1)}, f32[2,8,1024]{2,1,0:T(8,128)}) custom-call(s32[2]{0:T(128)} %counts_ref.3, bf16[2,512,768]{2,1,0:T(8,128)(2,1)} %tiles_ref.3, bf16[2,512,768]{2,1,0:T(8,128)(2,1)} %copy-done.2, bf16[768,768]{1,0:T(8,128)(2,1)} %wo_ref.1, f32[1,768]{1,0:T(1,128)} %reshape.11.gain_ref, bf16[768,3072]{1,0:T(8,128)(2,1)} %fi_ref.1, ...), custom_call_target="tpu_custom_call" | custom-call | flops 12079595520 | bytes 6291456 | tf_op jit(solution)/shard_map/pallas_call | solution.py:396
  114.4 19.3 %shard_map.115 = f32[2,8,768]{2,1,0:T(8,128)} custom-call(f32[2,8,1024]{2,1,0:T(8,128)} %get-tuple-element.5.stat_ref), custom_call_target="tpu_custom_call" | custom-call | tf_op jit(solution)/shard_map/pallas_call | solution.py:484
  133.7 1.4 %copy.13 = f32[2,8,768]{2,1,0:T(8,128)} copy(f32[2,8,768]{2,1,0:T(8,128)} %shard_map.115) | data formatting | bytes 98304
Async XLA Ops:
  7.2 84.3 %all-gather.2.cloned.1.call-start = ((), (), s32[]{:S(2)}) async-start(), calls=%async_computation | async-start | bytes 1474560 | tf_op jit(solution)/shard_map/all_gather | solution.py:511
  9.9 1.4 copy-start
  11.3 0.7 copy-start.1
  90.3 1.2 copy-start.2
Sparse Core Ops, SparseCore 0:
  9.8 30.4 all-gather.1
where the time goes:
time: 144 us; the launch traced here: 142 us
  Pallas kernels  121 us (84%)
  between operations  14.1 us (10%)
  local copies, waits for them, and re-layouts  6.59 us (5%)
    pallas_call x1, Pallas kernels, attention(): pl.pallas_call(functools.partial(attention_kernel, ratio), out_shape=jax....  78.4 us
    pallas_call x1, Pallas kernels, feed(): pl.pallas_call(feed_kernel, grid=(slides, rows // size), out_shape=(jax.S...  22.9 us
    pallas_call x1, Pallas kernels, pool(): pl.pallas_call(functools.partial(pool_kernel, ratio), out_shape=jax.Shape...  19.3 us
    unnamed x7, local copies, waits for them, and re-layouts  4.63 us
  transfers between devices with their start and end apart: 1, of which 0 were waited for; matrix products, arithmetic and copies ran while one was open for 1% of the time, Pallas kernels for 55%

commit v1 on v0

v1 whole, which is shorter than its diff:
```python
import functools
import math

import jax
import jax.numpy as jnp
from jax import lax
from jax.experimental import pallas as pl
from jax.experimental.pallas import tpu as pltpu
from jax.sharding import PartitionSpec as P

HEADS = 16
BLOCK = 256
AUG = 16
NEG = -1e30
NT = (((1,), (1,)), ((), ()))
TN = (((0,), (0,)), ((), ()))


def normalize(xf, gain):
    centre = jnp.mean(xf, axis=-1, keepdims=True)
    spread = jnp.mean((xf - centre) ** 2, axis=-1, keepdims=True)
    return (xf - centre) * lax.rsqrt(spread + 1e-05) * gain


def spread_matrix(rows, ratio):
    chunk = rows // ratio
    r = lax.broadcasted_iota(jnp.int32, (rows, rows), 0)
    t = lax.broadcasted_iota(jnp.int32, (rows, rows), 1)
    return jnp.where((r % chunk) * ratio + r // chunk == t, 1.0, 0.0)


def attend(kt, qt, vt, head_dim):
    scale = 1.0 / head_dim**0.5
    c = scale * math.log2(math.e)
    s = lax.dot_general(kt, qt, TN, preferred_element_type=jnp.float32)
    m = jnp.max(s, axis=0, keepdims=True)
    p = jnp.exp2((s - m) * c).astype(jnp.bfloat16)
    o = jnp.dot(vt, p, preferred_element_type=jnp.float32)
    total = o[head_dim : head_dim + 1]
    return o[:head_dim] / total, m * scale + jnp.log(total)


def gelu(x):
    return 0.5 * x * (1.0 + lax.erf(x * math.sqrt(0.5)))


def layer_kernel(
    ratio,
    counts_ref,
    tiles_hbm,
    gain_ref,
    gain2_ref,
    cw_ref,
    w_hbm,
    wo_hbm,
    fi_hbm,
    fo_hbm,
    pw_hbm,
    enc_ref,
    pooled_ref,
    tiles_ref,
    w_ref,
    wo_ref,
    fi_ref,
    fo_ref,
    pw_ref,
    wt,
    spread_ref,
    x_near,
    x_send,
    x_recv,
    proj,
    near_out,
    near_lse,
    o_t,
    l_t,
    o_send,
    o_recv,
    l_send,
    l_recv,
    l_rows,
    mixed_ref,
    stat,
    stat_recv,
    row_send,
    row_recv,
    x_ss,
    x_rs,
    o_ss,
    o_rs,
    l_ss,
    l_rs,
    s_ss,
    s_rs,
    r_ss,
    r_rs,
    t_sem,
    w_sem,
):
    me = lax.axis_index("seq")
    slides, rows, width = tiles_ref.shape
    head_dim = width // HEADS
    nblocks = rows // BLOCK
    chunk = rows // ratio
    classes = cw_ref.shape[0]
    tile_loads = [
        pltpu.make_async_copy(tiles_hbm.at[s], tiles_ref.at[s], t_sem.at[s]) for s in range(slides)
    ]
    pairs = (
        (w_hbm, w_ref),
        (wo_hbm, wo_ref),
        (fi_hbm, fi_ref),
        (fo_hbm, fo_ref),
        (pw_hbm, pw_ref),
    )
    loads = [pltpu.make_async_copy(a, b, w_sem.at[i]) for i, (a, b) in enumerate(pairs)]
    for load in tile_loads + loads:
        load.start()

    def x_copy(s, peer):
        return pltpu.make_async_remote_copy(
            src_ref=x_send.at[s, peer],
            dst_ref=x_recv.at[s, me],
            send_sem=x_ss.at[s, peer],
            recv_sem=x_rs.at[s, me],
            device_id={"seq": peer},
            device_id_type=pl.DeviceIdType.MESH,
        )

    def x_arrival(s, peer):
        return pltpu.make_async_remote_copy(
            src_ref=x_send.at[s, peer],
            dst_ref=x_recv.at[s, peer],
            send_sem=x_ss.at[s, peer],
            recv_sem=x_rs.at[s, peer],
            device_id={"seq": peer},
            device_id_type=pl.DeviceIdType.MESH,
        )

    def o_copy(s, peer, slot):
        return pltpu.make_async_remote_copy(
            src_ref=o_send.at[s, peer],
            dst_ref=o_recv.at[s, slot],
            send_sem=o_ss.at[s, peer],
            recv_sem=o_rs.at[s, slot],
            device_id={"seq": peer},
            device_id_type=pl.DeviceIdType.MESH,
        )

    def l_copy(s, peer, slot):
        return pltpu.make_async_remote_copy(
            src_ref=l_send.at[s, peer],
            dst_ref=l_recv.at[s, slot],
            send_sem=l_ss.at[s, peer],
            recv_sem=l_rs.at[s, slot],
            device_id={"seq": peer},
            device_id_type=pl.DeviceIdType.MESH,
        )

    def s_copy(s, owner, slot):
        return pltpu.make_async_remote_copy(
            src_ref=stat.at[s, owner],
            dst_ref=stat_recv.at[s, slot],
            send_sem=s_ss.at[s, owner],
            recv_sem=s_rs.at[s, slot],
            device_id={"seq": owner},
            device_id_type=pl.DeviceIdType.MESH,
        )

    def r_copy(peer, slot):
        return pltpu.make_async_remote_copy(
            src_ref=row_send,
            dst_ref=row_recv.at[slot],
            send_sem=r_ss.at[peer],
            recv_sem=r_rs.at[slot],
            device_id={"seq": peer},
            device_id_type=pl.DeviceIdType.MESH,
        )

    def partner(k):
        return lax.rem(me + k, ratio)

    barrier = pltpu.get_barrier_semaphore()
    for k in range(1, ratio):
        pl.semaphore_signal(
            barrier, inc=1, device_id={"seq": partner(k)}, device_id_type=pl.DeviceIdType.MESH
        )

    spread_ref[...] = spread_matrix(rows, ratio).astype(jnp.bfloat16)
    for s in range(slides):
        tile_loads[s].wait()
        xf = tiles_ref[s].astype(jnp.float32)
        normed = normalize(xf, gain_ref[...].reshape(1, width)).astype(jnp.bfloat16)
        x_near[s] = normed
        moved = jnp.dot(spread_ref[...], normed, preferred_element_type=jnp.float32)
        x_send[s] = moved.astype(jnp.bfloat16).reshape(ratio, chunk, width)
        if s == 0:
            pl.semaphore_wait(barrier, ratio - 1)

        def send(k, carry, s=s):
            x_copy(s, partner(k)).start()
            return carry

        lax.fori_loop(1, ratio, send, 0)

    loads[0].wait()
    for j in range(3):
        wt[j] = w_ref[:, j * width : (j + 1) * width].T
    first = lax.broadcasted_iota(jnp.int32, (AUG, rows), 0) == 0
    lane = lax.broadcasted_iota(jnp.int32, (AUG, rows), 1)
    ones = jnp.where(first, 1.0, 0.0).astype(jnp.bfloat16)
    for h in range(HEADS):
        proj[0, h, head_dim:, :] = ones
        proj[2, h, head_dim:, :] = ones

    def project(x, keep):
        bias = jnp.where(first & jnp.logical_not(keep), NEG, 0.0).astype(jnp.bfloat16)
        for h in range(HEADS):
            proj[1, h, head_dim:, :] = bias

        def part(j, carry):
            y = lax.dot_general(wt[j], x, NT, preferred_element_type=jnp.float32)
            proj[j, :, :head_dim, :] = y.astype(jnp.bfloat16).reshape(HEADS, head_dim, rows)
            return carry

        lax.fori_loop(0, 3, part, 0)

    local_pos = me * rows + lane

    def near(s, carry):
        project(x_near[s], local_pos < counts_ref[s])

        def head(h, carry):
            for b in range(nblocks):
                cols = slice(b * BLOCK, (b + 1) * BLOCK)
                out, lse = attend(
                    proj[1, h, :, cols], proj[0, h, :, cols], proj[2, h, :, cols], head_dim
                )
                near_out[s, h, :, cols] = out
                near_lse[s, h, :, cols] = lse
            return carry

        lax.fori_loop(0, HEADS, head, 0, unroll=4)
        return carry

    lax.fori_loop(0, slides, near, 0)

    class_pos = lane * ratio + me

    def far(s, carry):
        def arrive(k, carry):
            x_arrival(s, partner(k)).wait_recv()
            return carry

        lax.fori_loop(1, ratio, arrive, 0)
        x_recv[s, me] = x_send[s, me]
        project(x_recv[s].reshape(rows, width), class_pos < counts_ref[s])

        def head(h, carry):
            out, lse = attend(proj[1, h], proj[0, h], proj[2, h], head_dim)
            o_t[h] = out.astype(jnp.bfloat16)
            l_t[h] = lse
            return carry

        lax.fori_loop(0, HEADS, head, 0, unroll=2)
        o_send[s] = o_t[...].reshape(width, rows).T.reshape(ratio, chunk, width)
        lse = l_t[...].reshape(HEADS, rows)
        for d in range(ratio):
            l_send[s, d] = lse[:, d * chunk : (d + 1) * chunk]

        def send(k, carry):
            o_copy(s, partner(k), me).start()
            l_copy(s, partner(k), me).start()
            return carry

        lax.fori_loop(1, ratio, send, 0)
        return carry

    lax.fori_loop(0, slides, far, 0)

    def mix(s, carry):
        def arrive(k, carry):
            o_copy(s, partner(k), partner(k)).wait_recv()
            l_copy(s, partner(k), partner(k)).wait_recv()
            return carry

        lax.fori_loop(1, ratio, arrive, 0)
        o_recv[s, me] = o_send[s, me]
        l_recv[s, me] = l_send[s, me]
        for c in range(ratio):
            l_rows[c] = l_recv[s, c].T
        far_lse = jnp.dot(
            l_rows[...].reshape(rows, HEADS).T,
            spread_ref[...].astype(jnp.float32),
            precision=lax.Precision.HIGHEST,
            preferred_element_type=jnp.float32,
        ).reshape(HEADS, 1, rows)
        n_lse = near_lse[s]
        top = jnp.maximum(n_lse, far_lse)
        n_w = jnp.exp(n_lse - top)
        f_w = jnp.exp(far_lse - top)
        inv = 1.0 / (n_w + f_w)
        n_w = n_w * inv
        f_w = f_w * inv
        far_out = lax.dot_general(
            o_recv[s].reshape(rows, width),
            spread_ref[...],
            TN,
            preferred_element_type=jnp.float32,
        ).reshape(HEADS, head_dim, rows)
        mixed = (n_w * near_out[s] + f_w * far_out).astype(jnp.bfloat16)
        mixed_ref[...] = mixed.reshape(width, rows).T
        return carry

    def finish(s, carry):
        mix(s, carry)
        f32, bf16 = jnp.float32, jnp.bfloat16
        start = me * rows
        count = counts_ref[s]
        resid = tiles_ref[s].astype(f32) + jnp.dot(
            mixed_ref[...], wo_ref[...], preferred_element_type=f32
        )
        normed = normalize(resid, gain2_ref[...].reshape(1, width)).astype(bf16)
        ff = fi_ref.shape[1]
        step = width
        out = resid
        for j in range(0, ff, step):
            h = jnp.dot(normed, fi_ref[:, j : j + step], preferred_element_type=f32)
            act = gelu(h).astype(bf16)
            out = out + jnp.dot(act, fo_ref[j : j + step, :], preferred_element_type=f32)
        rowpos = start + lax.broadcasted_iota(jnp.int32, (rows, width), 0)
        encoded = jnp.where(rowpos < count, out, 0.0).astype(bf16)
        enc_ref[s] = encoded
        zed = jnp.dot(encoded, pw_ref[...], preferred_element_type=f32)
        hidden = zed.shape[1] // 2
        gate = jnp.tanh(zed[:, :hidden]) * jax.nn.sigmoid(zed[:, hidden:])
        logits = lax.dot_general(
            cw_ref[...], gate, NT, precision=lax.Precision.HIGHEST, preferred_element_type=f32
        )
        keep = start + lax.broadcasted_iota(jnp.int32, (classes, rows), 1) < count
        logits = jnp.where(keep, logits, NEG)

        peak = jnp.max(logits, axis=1, keepdims=True)
        expo = jnp.where(keep, jnp.exp(logits - peak), 0.0)
        numer = jnp.dot(
            expo, encoded.astype(f32), precision=lax.Precision.HIGHEST, preferred_element_type=f32
        )
        total = jnp.sum(expo, axis=1, keepdims=True)
        for c in range(classes):
            row = slice(c, c + 1)
            stat[s, c, :, :width] = numer[row]
            stat[s, c, :, width : width + 128] = jnp.broadcast_to(total[row], (1, 128))
            stat[s, c, :, width + 128 :] = jnp.broadcast_to(peak[row], (1, 128))

        def send(k, carry):
            @pl.when(partner(k) < classes)
            def _():
                s_copy(s, partner(k), me).start()

            return carry

        lax.fori_loop(1, ratio, send, 0)
        return carry

    for load in loads[1:]:
        load.wait()
    lax.fori_loop(0, slides, finish, 0)

    @pl.when(me < classes)
    def _():
        for s in range(slides):

            def arrive(k, carry, s=s):
                s_copy(s, me, partner(k)).wait_recv()
                return carry

            lax.fori_loop(1, ratio, arrive, 0)
            stat_recv[s, me] = stat[s, me]
            peaks = stat_recv[s, :, :, width + 128 :]
            fade = jnp.exp(peaks - jnp.max(peaks, axis=0, keepdims=True))
            inv = 1.0 / jnp.sum(stat_recv[s, :, :, width : width + 128] * fade, axis=0)
            for j in range(0, width, 128):
                numer = jnp.sum(stat_recv[s, :, :, j : j + 128] * fade, axis=0)
                row_send[s, :, j : j + 128] = numer * inv

        def send(k, carry):
            r_copy(partner(k), me).start()
            return carry

        lax.fori_loop(1, ratio, send, 0)
        row_recv[me] = row_send[...]

    def collect(k, carry):
        @pl.when(partner(k) < classes)
        def _():
            r_copy(partner(k), partner(k)).wait_recv()

        return carry

    lax.fori_loop(1, ratio, collect, 0)
    for c in range(classes):
        for s in range(slides):
            pooled_ref[s, c : c + 1, :] = row_recv[c, s]

    def drain(i, carry):
        s = i // (ratio - 1)
        peer = partner(i % (ratio - 1) + 1)
        x_copy(s, peer).wait_send()
        o_copy(s, peer, me).wait_send()
        l_copy(s, peer, me).wait_send()

        @pl.when(peer < classes)
        def _():
            s_copy(s, peer, me).wait_send()

        return carry

    lax.fori_loop(0, slides * (ratio - 1), drain, 0)

    @pl.when(me < classes)
    def _():
        def sent(k, carry):
            r_copy(partner(k), me).wait_send()
            return carry

        lax.fori_loop(1, ratio, sent, 0)


def layer(counts, tiles, gain, gain2, cw, w, wo, fi, fo, pw, ratio):
    slides, rows, width = tiles.shape
    head_dim = width // HEADS
    chunk = rows // ratio
    bf16, f32 = jnp.bfloat16, jnp.float32
    classes = cw.shape[0]
    vmem = pl.BlockSpec(memory_space=pltpu.VMEM)
    hbm = pl.BlockSpec(memory_space=pl.ANY)
    sem = pltpu.SemaphoreType.DMA((slides, ratio))
    return pl.pallas_call(
        functools.partial(layer_kernel, ratio),
        out_shape=(
            jax.ShapeDtypeStruct((slides, rows, width), bf16),
            jax.ShapeDtypeStruct((slides, classes, width), f32),
        ),
        in_specs=[pl.BlockSpec(memory_space=pltpu.SMEM), hbm, vmem, vmem, vmem] + [hbm] * 5,
        out_specs=(vmem, vmem),
        scratch_shapes=[
            pltpu.VMEM(tiles.shape, bf16),
            pltpu.VMEM(w.shape, bf16),
            pltpu.VMEM(wo.shape, bf16),
            pltpu.VMEM(fi.shape, bf16),
            pltpu.VMEM(fo.shape, bf16),
            pltpu.VMEM(pw.shape, bf16),
            pltpu.VMEM((3, width, width), bf16),
            pltpu.VMEM((rows, rows), bf16),
            pltpu.VMEM((slides, rows, width), bf16),
            pltpu.VMEM((slides, ratio, chunk, width), bf16),
            pltpu.VMEM((slides, ratio, chunk, width), bf16),
            pltpu.VMEM((3, HEADS, head_dim + AUG, rows), bf16),
            pltpu.VMEM((slides, HEADS, head_dim, rows), f32),
            pltpu.VMEM((slides, HEADS, 1, rows), f32),
            pltpu.VMEM((HEADS, head_dim, rows), bf16),
            pltpu.VMEM((HEADS, 1, rows), f32),
            pltpu.VMEM((slides, ratio, chunk, width), bf16),
            pltpu.VMEM((slides, ratio, chunk, width), bf16),
            pltpu.VMEM((slides, ratio, HEADS, chunk), f32),
            pltpu.VMEM((slides, ratio, HEADS, chunk), f32),
            pltpu.VMEM((ratio, chunk, HEADS), f32),
            pltpu.VMEM((rows, width), bf16),
            pltpu.VMEM((slides, classes, 1, width + 256), f32),
            pltpu.VMEM((slides, ratio, 1, width + 256), f32),
            pltpu.VMEM((slides, 1, width), f32),
            pltpu.VMEM((ratio, slides, 1, width), f32),
            sem,
            sem,
            sem,
            sem,
            sem,
            sem,
            sem,
            sem,
            pltpu.SemaphoreType.DMA((ratio,)),
            pltpu.SemaphoreType.DMA((ratio,)),
            pltpu.SemaphoreType.DMA((slides,)),
            pltpu.SemaphoreType.DMA((5,)),
        ],
        compiler_params=pltpu.CompilerParams(
            collective_id=0, has_side_effects=True, vmem_limit_bytes=60 * 2**20
        ),
        cost_estimate=pl.CostEstimate(
            flops=2 * slides * rows * width * width * 8,
            bytes_accessed=8 * slides * rows * width,
            transcendentals=0,
        ),
    )(counts, tiles, gain, gain2, cw, w, wo, fi, fo, pw)


def local(
    tiles,
    counts,
    ln1_gain,
    qkv_weight,
    out_weight,
    ln2_gain,
    ff_in,
    ff_out,
    pool_weight,
    class_weight,
):
    ratio = lax.axis_size("seq")
    pw = lax.all_gather(pool_weight, "grp", axis=0, tiled=True)
    return layer(
        counts,
        tiles,
        ln1_gain,
        ln2_gain,
        class_weight.T,
        qkv_weight,
        out_weight,
        ff_in,
        ff_out,
        pw,
        ratio,
    )


def solution(mesh):
    placed = (P("grp", "seq", None), P("grp"), P(), P(), P(), P(), P(), P(), P("grp", None), P())
    return jax.shard_map(
        local,
        mesh=mesh,
        in_specs=placed,
        out_specs=(P("grp", "seq", None), P("grp", None, None)),
        check_vma=False,
    )
```

time: 144 us -> 155 us (1.076)
  waiting for transfers between devices: 0.68 us -> 33.1 us
  Pallas kernels: 121 us -> 104 us
  local copies, waits for them, and re-layouts: 6.59 us -> 3.29 us
    all_gather x1, waiting for transfers between devices: 0.01 us -> 32.4 us  [local(): pw = lax.all_gather(pool_weight, 'grp', axis=0, tiled=True)]
    pallas_call x3 -> x1, Pallas kernels: 121 us -> 104 us  [layer(): pl.pallas_call(functools.partial(layer_kernel, ratio), out_shape=(jax.Sha...]
    reshape x2 -> x0, local copies, waits for them, and re-layouts: 1.96 us -> none  [the longest x1 1.27 us: feed(): gain = gain.reshape(1, width)]
    unnamed x7 -> x4, local copies, waits for them, and re-layouts: 4.63 us -> 3.29 us
  transfers between devices with their start and end apart: 1 -> 1, of which waited for: 0 -> 1; matrix products, arithmetic and copies ran while one was open for 1% -> 0% of each run, Pallas kernels for 55% -> 0%
where the time goes in v1:
time: 155 us; the launch traced here: 154 us
  Pallas kernels  104 us (67%)
  waiting for transfers between devices  33.1 us (21%)
  between operations  14 us (9%)
  local copies, waits for them, and re-layouts  3.29 us (2%)
    pallas_call x1, Pallas kernels, layer(): pl.pallas_call(functools.partial(layer_kernel, ratio), out_shape=(jax.Sha...  104 us
    all_gather x1, waiting for transfers between devices, local(): pw = lax.all_gather(pool_weight, 'grp', axis=0, tiled=True)  32.4 us
    unnamed x4, local copies, waits for them, and re-layouts  3.29 us
  transfers between devices with their start and end apart: 1, of which 1 were waited for; matrix products, arithmetic and copies ran while one was open for 0% of the time, Pallas kernels for 0%

profile of v1, /device:TPU:0, one launch (start us, length us, event | category | flops | bytes accessed | tf_op | source)
XLA Modules:
  0.0 154.3 jit_solution(6797801972212958167)
XLA Ops:
  7.2 0.0 all-gather.2.cloned.1.call-start
  7.2 0.7 all-gather.2.cloned.1.call-update
  7.9 32.4 %all-gather.2.cloned.1.call-done.pw_hbm = bf16[768,768]{1,0:T(8,128)(2,1)} async-done(((bf16[192,768]{1,0:T(8,128)(2,1)}), bf16[768,768]{1,0:T(8,128)(2,1)}) %all-gather.2.cloned.1.call-update) | async-done | bytes 1179664 | tf_op jit(solution)/shard_map/all_gather | solution.py:510
  40.3 103.9 %shard_map.113 = (bf16[2,512,768]{2,1,0:T(8,128)(2,1)}, f32[2,8,768]{2,1,0:T(8,128)}) custom-call(s32[2]{0:T(128)} %counts_ref.1, bf16[2,512,768]{2,1,0:T(8,128)(2,1)} %tiles_hbm.1, f32[768]{0:T(1024)} %gain_ref.1, f32[768]{0:T(1024)} %gain2_ref.1, f32[8,384]{1,0:T(8,128)} %bitcast.1, bf16[768,2304]{1,0:T(8,128)(2,1)} %w_hbm.1, bf16[768,768]{1,0:T(8,128)(2,1)} %wo_hbm.1, ...), custom_call_target="tpu_custom_call" | custom-call | flops 9663676416 | bytes 6291456 | tf_op jit(solution)/shard_map/pallas_call | solution.py:438
  144.2 0.0 copy-start
  144.2 2.7 %copy.14 = bf16[2,512,768]{2,1,0:T(8,128)(2,1)} copy(bf16[2,512,768]{2,1,0:T(8,128)(2,1)} %get-tuple-element.4) | data formatting | bytes 3145728
  146.8 0.0 copy-done
  146.8 0.6 copy.15
Async XLA Ops:
  7.2 33.1 %all-gather.2.cloned.1.call-start = ((), (), s32[]{:S(2)}) async-start(), calls=%async_computation | async-start | bytes 1474560 | tf_op jit(solution)/shard_map/all_gather | solution.py:510
  144.2 2.7 %copy-start = (f32[2,8,768]{2,1,0:T(8,128)S(1)}, f32[2,8,768]{2,1,0:T(8,128)}, u32[]{:S(2)}) copy-start(f32[2,8,768]{2,1,0:T(8,128)} %get-tuple-element.5) | copy-start | bytes 147460
Sparse Core Ops, SparseCore 0:
  9.8 30.4 all-gather.1

commit v2 on v1

--- a/solution.py
+++ b/solution.py
@@ -96,8 +96,12 @@
     r_rs,
     t_sem,
     w_sem,
+    pw_ss,
+    pw_rs,
 ):
     me = lax.axis_index("seq")
+    part_me = lax.axis_index("grp")
+    parts = pw_ref.shape[0]
     slides, rows, width = tiles_ref.shape
     head_dim = width // HEADS
     nblocks = rows // BLOCK
@@ -111,7 +115,7 @@
         (wo_hbm, wo_ref),
         (fi_hbm, fi_ref),
         (fo_hbm, fo_ref),
-        (pw_hbm, pw_ref),
+        (pw_hbm, pw_ref.at[part_me]),
     )
     loads = [pltpu.make_async_copy(a, b, w_sem.at[i]) for i, (a, b) in enumerate(pairs)]
     for load in tile_loads + loads:
@@ -180,10 +184,27 @@
     def partner(k):
         return lax.rem(me + k, ratio)
 
+    def part_partner(k):
+        return lax.rem(part_me + k, parts)
+
+    def w_copy(peer, slot):
+        return pltpu.make_async_remote_copy(
+            src_ref=pw_hbm,
+            dst_ref=pw_ref.at[slot],
+            send_sem=pw_ss.at[peer],
+            recv_sem=pw_rs.at[slot],
+            device_id={"grp": peer},
+            device_id_type=pl.DeviceIdType.MESH,
+        )
+
     barrier = pltpu.get_barrier_semaphore()
     for k in range(1, ratio):
         pl.semaphore_signal(
             barrier, inc=1, device_id={"seq": partner(k)}, device_id_type=pl.DeviceIdType.MESH
+        )
+    for k in range(1, parts):
+        pl.semaphore_signal(
+            barrier, inc=1, device_id={"grp": part_partner(k)}, device_id_type=pl.DeviceIdType.MESH
         )
 
     spread_ref[...] = spread_matrix(rows, ratio).astype(jnp.bfloat16)
@@ -195,13 +216,16 @@
         moved = jnp.dot(spread_ref[...], normed, preferred_element_type=jnp.float32)
         x_send[s] = moved.astype(jnp.bfloat16).reshape(ratio, chunk, width)
         if s == 0:
-            pl.semaphore_wait(barrier, ratio - 1)
+            pl.semaphore_wait(barrier, ratio - 1 + parts - 1)
 
         def send(k, carry, s=s):
             x_copy(s, partner(k)).start()
             return carry
 
         lax.fori_loop(1, ratio, send, 0)
+
+    for k in range(1, parts):
+        w_copy(part_partner(k), part_me).start()
 
     loads[0].wait()
     for j in range(3):
@@ -243,7 +267,7 @@
         lax.fori_loop(0, HEADS, head, 0, unroll=4)
         return carry
 
-    lax.fori_loop(0, slides, near, 0)
+    near(0, 0)
 
     class_pos = lane * ratio + me
 
@@ -277,6 +301,7 @@
         return carry
 
     lax.fori_loop(0, slides, far, 0)
+    lax.fori_loop(1, slides, near, 0)
 
     def mix(s, carry):
         def arrive(k, carry):
@@ -331,7 +356,7 @@
         rowpos = start + lax.broadcasted_iota(jnp.int32, (rows, width), 0)
         encoded = jnp.where(rowpos < count, out, 0.0).astype(bf16)
         enc_ref[s] = encoded
-        zed = jnp.dot(encoded, pw_ref[...], preferred_element_type=f32)
+        zed = jnp.dot(encoded, pw_ref[...].reshape(width, -1), preferred_element_type=f32)
         hidden = zed.shape[1] // 2
         gate = jnp.tanh(zed[:, :hidden]) * jax.nn.sigmoid(zed[:, hidden:])
         logits = lax.dot_general(
@@ -364,6 +389,8 @@
 
     for load in loads[1:]:
         load.wait()
+    for k in range(1, parts):
+        w_copy(part_partner(k), part_partner(k)).wait_recv()
     lax.fori_loop(0, slides, finish, 0)
 
     @pl.when(me < classes)
@@ -416,6 +443,8 @@
         return carry
 
     lax.fori_loop(0, slides * (ratio - 1), drain, 0)
+    for k in range(1, parts):
+        w_copy(part_partner(k), part_me).wait_send()
 
     @pl.when(me < classes)
     def _():
@@ -432,6 +461,7 @@
     chunk = rows // ratio
     bf16, f32 = jnp.bfloat16, jnp.float32
     classes = cw.shape[0]
+    parts = lax.axis_size("grp")
     vmem = pl.BlockSpec(memory_space=pltpu.VMEM)
     hbm = pl.BlockSpec(memory_space=pl.ANY)
     sem = pltpu.SemaphoreType.DMA((slides, ratio))
@@ -449,7 +479,7 @@
             pltpu.VMEM(wo.shape, bf16),
             pltpu.VMEM(fi.shape, bf16),
             pltpu.VMEM(fo.shape, bf16),
-            pltpu.VMEM(pw.shape, bf16),
+            pltpu.VMEM((parts,) + pw.shape, bf16),
             pltpu.VMEM((3, width, width), bf16),
             pltpu.VMEM((rows, rows), bf16),
             pltpu.VMEM((slides, rows, width), bf16),
@@ -482,9 +512,11 @@
             pltpu.SemaphoreType.DMA((ratio,)),
             pltpu.SemaphoreType.DMA((slides,)),
             pltpu.SemaphoreType.DMA((5,)),
+            pltpu.SemaphoreType.DMA((parts,)),
+            pltpu.SemaphoreType.DMA((parts,)),
         ],
         compiler_params=pltpu.CompilerParams(
-            collective_id=0, has_side_effects=True, vmem_limit_bytes=60 * 2**20
+            collective_id=0, has_side_effects=True, vmem_limit_bytes=48 * 2**20
         ),
         cost_estimate=pl.CostEstimate(
             flops=2 * slides * rows * width * width * 8,
@@ -507,7 +539,6 @@
     class_weight,
 ):
     ratio = lax.axis_size("seq")
-    pw = lax.all_gather(pool_weight, "grp", axis=0, tiled=True)
     return layer(
         counts,
         tiles,
@@ -518,7 +549,7 @@
         out_weight,
         ff_in,
         ff_out,
-        pw,
+        pool_weight,
         ratio,
     )
 

time: 155 us -> 112 us (0.72)
  waiting for transfers between devices: 33.1 us -> 0 us
  between operations: 14 us -> 0.66 us
  local copies, waits for them, and re-layouts: 3.29 us -> 8.13 us
    all_gather x1 -> x0, waiting for transfers between devices: 32.4 us -> none  [local(): pw = lax.all_gather(pool_weight, 'grp', axis=0, tiled=True)]
    unnamed x4 -> x16, local copies, waits for them, and re-layouts: 3.29 us -> 8.13 us
  transfers between devices with their start and end apart: 1 -> 0, of which waited for: 1 -> 0; matrix products, arithmetic and copies ran while one was open for 0% -> 0% of each run, Pallas kernels for 0% -> 0%
where the time goes in v2:
time: 112 us
  Pallas kernels  103 us (92%)
  local copies, waits for them, and re-layouts  8.13 us (7%)
    pallas_call x1, Pallas kernels, layer(): pl.pallas_call(functools.partial(layer_kernel, ratio), out_shape=(jax.Sha...  103 us
    unnamed x16, local copies, waits for them, and re-layouts  8.13 us

profile of v2, /device:TPU:0, one launch (start us, length us, event | category | flops | bytes accessed | tf_op | source)
XLA Modules:
  0.0 111.7 jit_solution(13341135977304902893)
XLA Ops:
  0.6 0.0 copy-start
  0.6 1.4 %copy-done = bf16[2,512,768]{2,1,0:T(8,128)(2,1)S(1)} copy-done((bf16[2,512,768]{2,1,0:T(8,128)(2,1)S(1)}, bf16[2,512,768]{2,1,0:T(8,128)(2,1)}, u32[]{:S(2)}) %copy-start) | copy-done | bytes 1572888
  2.0 0.0 copy-start.1
  2.0 1.3 %copy-done.1 = bf16[768,768]{1,0:T(8,128)(2,1)S(1)} copy-done((bf16[768,768]{1,0:T(8,128)(2,1)S(1)}, bf16[768,768]{1,0:T(8,128)(2,1)}, u32[]{:S(2)}) %copy-start.1) | copy-done | bytes 1179672
  3.3 0.0 copy-start.2
  3.3 1.0 copy-done.2
  4.3 0.0 copy-start.3
  4.3 0.7 copy-done.3
  5.0 0.0 copy-start.4
  5.0 0.7 copy-done.4
  5.7 0.0 copy-start.5
  5.7 0.7 copy-done.5
  6.4 0.0 copy-start.6
  6.4 0.7 copy-done.6
  7.0 102.9 %shard_map.113 = (bf16[2,512,768]{2,1,0:T(8,128)(2,1)S(1)}, f32[2,8,768]{2,1,0:T(8,128)S(1)}) custom-call(s32[2]{0:T(128)S(1)} %copy-done.6, bf16[2,512,768]{2,1,0:T(8,128)(2,1)S(1)} %copy-done, f32[768]{0:T(1024)S(1)} %copy-done.4, f32[768]{0:T(1024)S(1)} %copy-done.5, f32[8,384]{1,0:T(8,128)S(1)} %bitcast.1, bf16[768,2304]{1,0:T(8,128)(2,1)} %w_hbm.1, ...), custom_call_target="tpu_custom_call" | custom-call | flops 9663676416 | bytes 6291456 | tf_op jit(solution)/shard_map/pallas_call | solution.py:468
  109.9 1.1 %copy.14 = bf16[2,512,768]{2,1,0:T(8,128)(2,1)} copy(bf16[2,512,768]{2,1,0:T(8,128)(2,1)S(1)} %get-tuple-element.4) | data formatting | bytes 3145728
  111.0 0.6 copy.15
Async XLA Ops:
  0.6 1.4 %copy-start = (bf16[2,512,768]{2,1,0:T(8,128)(2,1)S(1)}, bf16[2,512,768]{2,1,0:T(8,128)(2,1)}, u32[]{:S(2)}) copy-start(bf16[2,512,768]{2,1,0:T(8,128)(2,1)} %tiles_hbm.1) | copy-start | bytes 4718596
  2.0 1.3 %copy-start.1 = (bf16[768,768]{1,0:T(8,128)(2,1)S(1)}, bf16[768,768]{1,0:T(8,128)(2,1)}, u32[]{:S(2)}) copy-start(bf16[768,768]{1,0:T(8,128)(2,1)} %wo_hbm.1) | copy-start | bytes 3538948
  3.3 1.0 copy-start.2
  4.3 0.7 copy-start.3
  5.0 0.7 copy-start.4
  5.7 0.7 copy-start.5
  6.4 0.7 copy-start.6
